TPU v7x, 256 devices: a whole 4x4x8 slice. The times are simulated.
256 devices in a mesh: lon: 32 (over x_hi, z, core), ch: 8 (over x_lo, y).
Axes of the slice: x: 4 (x_hi: 2, x_lo: 2; x = x_hi * 2 + x_lo), y: 4, z: 8, core: 2. Of those that a mesh axis runs over, the one named last changes fastest.
Arguments:
- field_state: bfloat16 [1440, 512, 256], P('lon', 'ch'), may hold values from -6 to 6
- zonal_taps: bfloat16 [256, 1440], replicated, may hold values from -0.15625 to 0.15625
- channel_mix: bfloat16 [512, 512], replicated, may hold values from -0.25 to 0.25
- channel_bias: float32 [512], replicated, may hold values from -3 to 3
Outputs:
- activated: bfloat16 [1440, 512, 256], P('lon', 'ch')
All inputs are finite; a program needn't handle non-finite values.
Results may differ from a plain program's by a relative error of at most 0.0047.
Values may be sent and summed in bfloat16 or wider, within the bound.
No kernel may reach another device: no remote copies, remote signals or barrier semaphores. Data moves between devices by JAX's collectives and lax.ppermute only.
A program may use at most 64 MiB of HBM per device.

v0:
```python
import jax
import jax.numpy as jnp
from jax import lax
from jax.experimental import pallas as pl
from jax.experimental.pallas import tpu as pltpu
from jax.sharding import PartitionSpec as P

HALF = 23
ROWS = 24
LIMIT = 40 * 1024 * 1024


def params():
    return pltpu.CompilerParams(vmem_limit_bytes=LIMIT)


def identity(n):
    rows = lax.broadcasted_iota(jnp.int32, (n, n), 0)
    columns = lax.broadcasted_iota(jnp.int32, (n, n), 1)
    return jnp.where(rows == columns, 1.0, 0.0).astype(jnp.bfloat16)


def times_transposed(a, b):
    return lax.dot_general(a, b, (((1,), (1,)), ((), ())), preferred_element_type=jnp.float32)


def pack_kernel(width, depth, x_ref, out_ref, wide):
    lats = x_ref.shape[1]
    eye = identity(lats)
    for r in range(HALF):
        low = x_ref[r * depth : (r + 1) * depth, :]
        if HALF + r < width:
            high = x_ref[(HALF + r) * depth : (HALF + r + 1) * depth, :]
        else:
            high = jnp.zeros_like(low)
        wide[pl.ds(r, lats, stride=ROWS), :] = times_transposed(eye, jnp.concatenate([low, high], 0))
    for r in range(HALF, ROWS):
        wide[pl.ds(r, lats, stride=ROWS), :] = jnp.zeros((lats, 2 * depth), jnp.float32)
    out_ref[...] = wide[...].astype(out_ref.dtype)


def unpack_kernel(width, depth, y_ref, out_ref, wide):
    lats = out_ref.shape[1]
    eye = identity(2 * depth)
    wide[...] = y_ref[...].astype(jnp.float32)
    for r in range(HALF):
        rows = wide[pl.ds(r, lats, stride=ROWS), :].astype(jnp.bfloat16)
        turned = times_transposed(eye, rows).astype(out_ref.dtype)
        out_ref[r * depth : (r + 1) * depth, :] = turned[:depth]
        if HALF + r < width:
            out_ref[(HALF + r) * depth : (HALF + r + 1) * depth, :] = turned[depth:]


def toeplitz_kernel(shifts_ref, out_ref):
    tall, long = out_ref.shape
    base = jnp.broadcast_to(shifts_ref[...].astype(jnp.float32), (tall, shifts_ref.shape[1]))
    rolled = pltpu.roll(base, 0, 1, stride=1, stride_axis=0)
    out_ref[...] = rolled[:, tall:].astype(out_ref.dtype)


def compute_kernel(lon_count, ch_count, width, length, x_ref, t_ref, mix_ref, bias_ref, out_ref, state, packed, result):
    channels = state.shape[1]
    tall = t_ref.shape[0]
    half_lanes = 64
    low = lax.broadcasted_iota(jnp.int32, (ROWS, 128), 1) < half_lanes
    for l in range(lon_count):
        for pair in range(ch_count // 2):
            at = (l * ch_count + 2 * pair) * ROWS
            first = x_ref[at : at + ROWS, :].astype(jnp.float32)
            second = x_ref[at + ROWS : at + 2 * ROWS, :].astype(jnp.float32)
            lanes = slice(pair * 128, (pair + 1) * 128)
            state[l * width : l * width + ROWS, lanes] = jnp.where(low, first, pltpu.roll(second, half_lanes, 1))
            state[l * width + HALF : l * width + HALF + ROWS, lanes] = jnp.where(
                low, pltpu.roll(first, half_lanes, 1), second
            )
    padded = state.shape[0]
    packed[...] = state[...].astype(jnp.bfloat16)
    packed[length:, :] = jnp.zeros((padded - length, channels), jnp.bfloat16)
    result[length:, :] = jnp.zeros((result.shape[0] - length, channels), jnp.float32)
    blocks = (length + tall - 1) // tall
    for block in range(blocks):
        start = block * tall
        count = min(tall, length - start)
        offset = (length // 128) * 128 - start
        taps = t_ref[:count, offset : offset + padded]
        filtered = jnp.dot(taps, packed[...], preferred_element_type=jnp.float32).astype(jnp.bfloat16)
        mixed = jnp.dot(filtered, mix_ref[...], preferred_element_type=jnp.float32) + bias_ref[...]
        result[start : start + count, :] = mixed / (1.0 + jnp.exp(-mixed))
    for l in range(lon_count):
        for pair in range(ch_count // 2):
            lanes = slice(pair * 128, (pair + 1) * 128)
            first = result[l * width : l * width + ROWS, lanes]
            second = result[l * width + HALF : l * width + HALF + ROWS, lanes]
            at = (l * ch_count + 2 * pair) * ROWS
            out_ref[at : at + ROWS, :] = jnp.where(low, first, pltpu.roll(second, half_lanes, 1)).astype(out_ref.dtype)
            out_ref[at + ROWS : at + 2 * ROWS, :] = jnp.where(low, pltpu.roll(first, half_lanes, 1), second).astype(
                out_ref.dtype
            )


def exchange(x):
    return lax.all_to_all(x, ("lon", "ch"), split_axis=0, concat_axis=0, tiled=True)


def body(field_state, zonal_taps, channel_mix, channel_bias):
    lon_count = lax.axis_size("lon")
    ch_count = lax.axis_size("ch")
    width, depth, lats = field_state.shape
    length = zonal_taps.shape[1]
    channels = channel_mix.shape[0]
    tall = 256
    padded = -(-length // 128) * 128
    whole = (length // 128) * 128
    long = whole + padded
    sent = pl.pallas_call(
        lambda *refs: pack_kernel(width, depth, *refs),
        out_shape=jax.ShapeDtypeStruct((lats * ROWS, 2 * depth), jnp.bfloat16),
        scratch_shapes=[pltpu.VMEM((lats * ROWS, 2 * depth), jnp.float32)],
        compiler_params=params(),
        name="pack",
    )(field_state.reshape(width * depth, lats))
    mine = lax.axis_index("lon") * ch_count + lax.axis_index("ch")
    row = lax.dynamic_slice_in_dim(zonal_taps, mine, 1, 0)
    turned = jnp.flip(row, 1)
    start = (length - 1 - whole - tall) % length
    shifts = jnp.concatenate([turned[:, start:], turned, turned, turned], 1)[:, : long + tall]
    strip = pl.pallas_call(
        toeplitz_kernel,
        out_shape=jax.ShapeDtypeStruct((tall, long), jnp.bfloat16),
        compiler_params=params(),
        name="toeplitz",
    )(shifts)
    got = exchange(sent.reshape(lats, ROWS, 2 * depth)).reshape(lats * ROWS, 2 * depth)
    answer = pl.pallas_call(
        lambda *refs: compute_kernel(lon_count, ch_count, width, length, *refs),
        out_shape=jax.ShapeDtypeStruct((lats * ROWS, 2 * depth), jnp.bfloat16),
        scratch_shapes=[
            pltpu.VMEM((padded, channels), jnp.float32),
            pltpu.VMEM((padded, channels), jnp.bfloat16),
            pltpu.VMEM((padded, channels), jnp.float32),
        ],
        compiler_params=params(),
        name="filter_mix",
    )(got, strip, channel_mix, channel_bias.reshape(1, channels))
    back = exchange(answer.reshape(lats, ROWS, 2 * depth)).reshape(lats * ROWS, 2 * depth)
    out = pl.pallas_call(
        lambda *refs: unpack_kernel(width, depth, *refs),
        out_shape=jax.ShapeDtypeStruct((width * depth, lats), jnp.bfloat16),
        scratch_shapes=[pltpu.VMEM((lats * ROWS, 2 * depth), jnp.float32)],
        compiler_params=params(),
        name="unpack",
    )(back)
    return out.reshape(width, depth, lats)


def solution(mesh):
    placed = (P("lon", "ch", None), P(), P(), P())
    return jax.shard_map(
        body, mesh=mesh, in_specs=placed, out_specs=P("lon", "ch", None), check_vma=False
    )
```

profile of v0, /device:TPU:1, one launch (start us, length us, event | category | flops | bytes accessed | tf_op | source)
XLA Modules:
  0.0 117.9 jit_solution(16943583959230713575)
XLA Ops:
  0.0 0.0 copy-start
  0.0 0.0 copy-start.3
  0.0 1.4 %copy-done.3 = bf16[45,64,256]{2,1,0:T(8,128)(2,1)S(1)} copy-done((bf16[45,64,256]{2,1,0:T(8,128)(2,1)S(1)}, bf16[45,64,256]{2,1,0:T(8,128)(2,1)}, u32[]{:S(2)}) %copy-start.3) | copy-done | bytes 1474584
  1.4 2.2 %pack.1 = bf16[6144,128]{1,0:T(8,128)(2,1)} custom-call(bf16[2880,256]{1,0:T(8,128)(2,1)S(1)} %bitcast.12), custom_call_target="tpu_custom_call" | custom-call | tf_op jit(solution)/shard_map/pack/pallas_call | solution.py:115
  3.7 15.7 %all-to-all-start = ((bf16[256,24,128]{2,1,0:T(8,128)(2,1)}), bf16[256,24,128]{2,1,0:T(8,128)(2,1)S(1)}, u32[]{:S(2)}, u32[]{:S(2)}) async-start(bf16[256,24,128]{2,1,0:T(8,128)(2,1)} %bitcast.1), calls=%async_computation | async-start | bytes 3145728 | tf_op jit(solution)/shard_map/all_to_all | solution.py:102
  19.3 0.0 copy-start.4
  19.3 0.0 copy-start.5
  19.3 0.0 copy-done
  19.4 0.2 constant_dynamic-slice_fusion
  19.5 0.2 copy.6
  19.7 0.2 reverse.1
  19.9 0.1 slice.14
  20.0 1.1 reverse.2
  21.1 0.1 slice.15
  21.2 0.1 concatenate.3
  21.3 0.3 toeplitz.1.refs_1_
  21.6 0.0 copy-start.1
  21.6 1.1 copy-done.1
  22.8 38.6 %all-to-all-done = bf16[256,24,128]{2,1,0:T(8,128)(2,1)S(1)} async-done(((bf16[256,24,128]{2,1,0:T(8,128)(2,1)}), bf16[256,24,128]{2,1,0:T(8,128)(2,1)S(1)}, u32[]{:S(2)}, u32[]{:S(2)}) %all-to-all-start) | async-done | bytes 1572896 | tf_op jit(solution)/shard_map/all_to_all | solution.py:102
  61.4 0.0 copy-done.4
  61.4 0.0 copy-done.5
  61.4 0.0 copy-start.2
  61.4 1.4 %copy-done.2 = bf16[256,2944]{1,0:T(8,128)(2,1)S(1)} copy-done((bf16[256,2944]{1,0:T(8,128)(2,1)S(1)}, bf16[256,2944]{1,0:T(8,128)(2,1)}, u32[]{:S(2)}) %copy-start.2) | copy-done | bytes 1507352
  62.8 4.7 %filter_mix.1 = bf16[6144,128]{1,0:T(8,128)(2,1)S(1)} custom-call(bf16[6144,128]{1,0:T(8,128)(2,1)S(1)} %bitcast.10, bf16[256,2944]{1,0:T(8,128)(2,1)S(1)} %copy-done.2, bf16[512,512]{1,0:T(8,128)(2,1)S(1)} %copy-done.4, f32[1,512]{1,0:T(1,128)S(1)} %bitcast.13), custom_call_target="tpu_custom_call" | custom-call | tf_op jit(solution)/shard_map/filter_mix/pallas_call | solution.py:134
  67.5 48.3 %all_to_all.10 = bf16[256,24,128]{2,1,0:T(8,128)(2,1)S(1)} all-to-all(bf16[256,24,128]{2,1,0:T(8,128)(2,1)S(1)} %bitcast.11), channel_id=1, replica_groups=mesh['lon'=32,'ch'=8] {'lon','ch'}, dimensions={0} | all-to-all | bytes 3145728 | tf_op jit(solution)/shard_map/all_to_all | solution.py:102
  115.8 2.0 %unpack.1 = bf16[2880,256]{1,0:T(8,128)(2,1)} custom-call(bf16[6144,128]{1,0:T(8,128)(2,1)S(1)} %bitcast.9), custom_call_target="tpu_custom_call" | custom-call | tf_op jit(solution)/shard_map/unpack/pallas_call | solution.py:146
  (2 shorter events, 0.0 us)
Async XLA Ops:
  0.0 19.3 %copy-start = (bf16[256,1440]{0,1:T(8,128)(2,1)S(1)}, bf16[256,1440]{0,1:T(8,128)(2,1)}, u32[]{:S(2)}) copy-start(bf16[256,1440]{0,1:T(8,128)(2,1)} %param.5) | copy-start | bytes 2211844
  0.0 1.4 %copy-start.3 = (bf16[45,64,256]{2,1,0:T(8,128)(2,1)S(1)}, bf16[45,64,256]{2,1,0:T(8,128)(2,1)}, u32[]{:S(2)}) copy-start(bf16[45,64,256]{2,1,0:T(8,128)(2,1)} %param.4) | copy-start | bytes 4423684
  3.7 57.7 %all-to-all-start = ((bf16[256,24,128]{2,1,0:T(8,128)(2,1)}), bf16[256,24,128]{2,1,0:T(8,128)(2,1)S(1)}, u32[]{:S(2)}, u32[]{:S(2)}) async-start(bf16[256,24,128]{2,1,0:T(8,128)(2,1)} %bitcast.1), calls=%async_computation | async-start | bytes 3145728 | tf_op jit(solution)/shard_map/all_to_all | solution.py:102
  19.3 42.1 %copy-start.4 = (bf16[512,512]{1,0:T(8,128)(2,1)S(1)}, bf16[512,512]{1,0:T(8,128)(2,1)}, u32[]{:S(2)}) copy-start(bf16[512,512]{1,0:T(8,128)(2,1)} %refs_2_.1) | copy-start | bytes 1572868
  19.3 42.1 %copy-start.5 = (f32[512]{0:T(512)S(1)}, f32[512]{0:T(512)}, u32[]{:S(2)}) copy-start(f32[512]{0:T(512)} %param.7) | copy-start | bytes 6148
  21.6 1.1 copy-start.1
  61.4 1.4 %copy-start.2 = (bf16[256,2944]{1,0:T(8,128)(2,1)S(1)}, bf16[256,2944]{1,0:T(8,128)(2,1)}, u32[]{:S(2)}) copy-start(bf16[256,2944]{1,0:T(8,128)(2,1)} %copy-done.1) | copy-start | bytes 4521988
where the time goes:
time: 118 us
  blocking collectives  48.3 us (41%)
  waiting for transfers between devices  38.6 us (33%)
  starting transfers between devices  15.7 us (13%)
  Pallas kernels  9.26 us (8%)
  local copies, waits for them, and re-layouts  5.93 us (5%)
    all_to_all x1, blocking collectives, exchange(): lax.all_to_all(x, ('lon', 'ch'), split_axis=0, concat_axis=0, tiled=True)  48.3 us
    all_to_all x1, waiting for transfers between devices, exchange(): lax.all_to_all(x, ('lon', 'ch'), split_axis=0, concat_axis=0, tiled=True)  38.6 us
    all_to_all x1, starting transfers between devices, exchange(): lax.all_to_all(x, ('lon', 'ch'), split_axis=0, concat_axis=0, tiled=True)  15.7 us
    unnamed x17, local copies, waits for them, and re-layouts  5.6 us
    pallas_call x1, Pallas kernels, body(): pl.pallas_call(lambda *refs: compute_kernel(lon_count, ch_count, width, l...  4.72 us
  transfers between devices with their start and end apart: 1, of which 1 were waited for; matrix products, arithmetic and copies ran while one was open for 2% of the time, Pallas kernels for 0%

commit v1 on v0

v1 whole, which is shorter than its diff:
```python
import jax
import jax.numpy as jnp
from jax import lax
from jax.experimental import pallas as pl
from jax.experimental.pallas import tpu as pltpu
from jax.sharding import PartitionSpec as P

HALF = 23
ROWS = 24
TALL = 256
LIMIT = 40 * 1024 * 1024
PIECES = 4


def params():
    return pltpu.CompilerParams(vmem_limit_bytes=LIMIT)


def identity(n):
    rows = lax.broadcasted_iota(jnp.int32, (n, n), 0)
    columns = lax.broadcasted_iota(jnp.int32, (n, n), 1)
    return jnp.where(rows == columns, 1.0, 0.0).astype(jnp.bfloat16)


def times_transposed(a, b):
    return lax.dot_general(a, b, (((1,), (1,)), ((), ())), preferred_element_type=jnp.float32)


def padded_length(length):
    return -(-length // 128) * 128


def strip_width(length):
    return (length // 128) * 128 + padded_length(length)


def periodic_reversed(row, length):
    padded = padded_length(length)
    whole = (length // 128) * 128
    chunks = padded // 128
    stacked = jnp.concatenate([row[:, c * 128 : (c + 1) * 128] for c in range(chunks)], 0)
    i = lax.broadcasted_iota(jnp.int32, (128, 128), 0)
    j = lax.broadcasted_iota(jnp.int32, (128, 128), 1)
    swap = jnp.where(i + j == 127, 1.0, 0.0).astype(jnp.bfloat16)
    flipped = jnp.dot(stacked.astype(jnp.bfloat16), swap, preferred_element_type=jnp.float32)
    width = strip_width(length) + TALL
    pieces = [flipped[c : c + 1, :] for c in range(chunks - 1, -1, -1)]
    pieces.append(jnp.zeros((1, width - padded), jnp.float32))
    line = jnp.broadcast_to(jnp.concatenate(pieces, 1), (8, width))
    column = lax.broadcasted_iota(jnp.int32, (8, width), 1)
    first = (whole + TALL + 1) % length - length
    result = jnp.zeros((8, width), jnp.float32)
    for start in range(first, width, length):
        shift = (start - (padded - length)) % width
        inside = (column >= start) & (column < start + length)
        result = jnp.where(inside, pltpu.roll(line, shift, 1), result)
    return result


def pack_kernel(width, depth, x_ref, out_ref, wide):
    lats = x_ref.shape[1]
    eye = identity(lats)
    for r in range(HALF):
        low = x_ref[r * depth : (r + 1) * depth, :]
        if HALF + r < width:
            high = x_ref[(HALF + r) * depth : (HALF + r + 1) * depth, :]
        else:
            high = jnp.zeros_like(low)
        wide[pl.ds(r, lats, stride=ROWS), :] = times_transposed(eye, jnp.concatenate([low, high], 0))
    for r in range(HALF, ROWS):
        wide[pl.ds(r, lats, stride=ROWS), :] = jnp.zeros((lats, 2 * depth), jnp.float32)
    out_ref[...] = wide[...].astype(out_ref.dtype)


def unpack_kernel(width, depth, y_ref, out_hbm, out_ref, wide, sems):
    lats = out_ref.shape[1]
    eye = identity(2 * depth)
    wide[...] = y_ref[...].astype(jnp.float32)
    step = -(-HALF // PIECES)
    copies = []
    for p in range(PIECES):
        a, b = min(p * step, HALF), min((p + 1) * step, HALF)
        for r in range(a, b):
            rows = wide[pl.ds(r, lats, stride=ROWS), :].astype(jnp.bfloat16)
            turned = times_transposed(eye, rows).astype(out_ref.dtype)
            out_ref[r * depth : (r + 1) * depth, :] = turned[:depth]
            if HALF + r < width:
                out_ref[(HALF + r) * depth : (HALF + r + 1) * depth, :] = turned[depth:]
        for side in range(2):
            rows = slice((side * HALF + a) * depth, min(side * HALF + b, width) * depth)
            copy = pltpu.make_async_copy(out_ref.at[rows, :], out_hbm.at[rows, :], sems.at[2 * p + side])
            copy.start()
            copies.append(copy)
    for copy in copies:
        copy.wait()


def filter_kernel(
    lon_count, ch_count, width, length, x_ref, turned_ref, mix_ref, bias_ref, out_ref, strip, state, packed, result
):
    channels = state.shape[1]
    half_lanes = 64
    me = lax.axis_index("lon") * ch_count + lax.axis_index("ch")
    chosen = lax.broadcasted_iota(jnp.int32, (16, turned_ref.shape[1]), 1) == me
    row = times_transposed(jnp.where(chosen, 1.0, 0.0).astype(jnp.bfloat16), turned_ref[...])[0:1]
    row = jnp.concatenate([row, jnp.zeros((1, padded_length(length) - length), jnp.float32)], 1)
    line = periodic_reversed(row, length)
    base = jnp.broadcast_to(line[0:1, :], (TALL, line.shape[1]))
    strip[...] = pltpu.roll(base, 0, 1, stride=1, stride_axis=0)[:, TALL:].astype(strip.dtype)
    low = lax.broadcasted_iota(jnp.int32, (ROWS, 128), 1) < half_lanes
    for l in range(lon_count):
        for pair in range(ch_count // 2):
            at = (l * ch_count + 2 * pair) * ROWS
            first = x_ref[at : at + ROWS, :].astype(jnp.float32)
            second = x_ref[at + ROWS : at + 2 * ROWS, :].astype(jnp.float32)
            lanes = slice(pair * 128, (pair + 1) * 128)
            state[l * width : l * width + ROWS, lanes] = jnp.where(low, first, pltpu.roll(second, half_lanes, 1))
            state[l * width + HALF : l * width + HALF + ROWS, lanes] = jnp.where(
                low, pltpu.roll(first, half_lanes, 1), second
            )
    padded = state.shape[0]
    packed[...] = state[...].astype(jnp.bfloat16)
    packed[length:, :] = jnp.zeros((padded - length, channels), jnp.bfloat16)
    result[length:, :] = jnp.zeros((result.shape[0] - length, channels), jnp.float32)
    for start in range(0, length, TALL):
        count = min(TALL, length - start)
        offset = (length // 128) * 128 - start
        taps = strip[:count, offset : offset + padded]
        filtered = jnp.dot(taps, packed[...], preferred_element_type=jnp.float32).astype(jnp.bfloat16)
        mixed = jnp.dot(filtered, mix_ref[...], preferred_element_type=jnp.float32) + bias_ref[...]
        result[start : start + count, :] = mixed / (1.0 + jnp.exp(-mixed))
    for l in range(lon_count):
        for pair in range(ch_count // 2):
            lanes = slice(pair * 128, (pair + 1) * 128)
            first = result[l * width : l * width + ROWS, lanes]
            second = result[l * width + HALF : l * width + HALF + ROWS, lanes]
            at = (l * ch_count + 2 * pair) * ROWS
            out_ref[at : at + ROWS, :] = jnp.where(low, first, pltpu.roll(second, half_lanes, 1)).astype(out_ref.dtype)
            out_ref[at + ROWS : at + 2 * ROWS, :] = jnp.where(low, pltpu.roll(first, half_lanes, 1), second).astype(
                out_ref.dtype
            )


def exchange(x):
    return lax.all_to_all(x, ("lon", "ch"), split_axis=0, concat_axis=0, tiled=True)


def pack(field, width, depth):
    lats = field.shape[1]
    return pl.pallas_call(
        lambda *refs: pack_kernel(width, depth, *refs),
        out_shape=jax.ShapeDtypeStruct((lats * ROWS, 2 * depth), jnp.bfloat16),
        scratch_shapes=[pltpu.VMEM((lats * ROWS, 2 * depth), jnp.float32)],
        compiler_params=params(),
        name="pack",
    )(field)


def filter_mix(got, zonal_taps, channel_mix, channel_bias, lon_count, ch_count, width):
    channels = channel_mix.shape[0]
    length = zonal_taps.shape[1]
    padded = padded_length(length)
    return pl.pallas_call(
        lambda *refs: filter_kernel(lon_count, ch_count, width, length, *refs),
        out_shape=jax.ShapeDtypeStruct(got.shape, jnp.bfloat16),
        scratch_shapes=[
            pltpu.VMEM((TALL, strip_width(length)), jnp.bfloat16),
            pltpu.VMEM((padded, channels), jnp.float32),
            pltpu.VMEM((padded, channels), jnp.bfloat16),
            pltpu.VMEM((padded, channels), jnp.float32),
        ],
        compiler_params=params(),
        name="filter_mix",
    )(got, zonal_taps.T, channel_mix, channel_bias.reshape(1, channels))


def unpack(back, width, depth, lats):
    return pl.pallas_call(
        lambda *refs: unpack_kernel(width, depth, *refs),
        out_shape=jax.ShapeDtypeStruct((width * depth, lats), jnp.bfloat16),
        out_specs=pl.BlockSpec(memory_space=pltpu.HBM),
        scratch_shapes=[
            pltpu.VMEM((width * depth, lats), jnp.bfloat16),
            pltpu.VMEM((lats * ROWS, 2 * depth), jnp.float32),
            pltpu.SemaphoreType.DMA((2 * PIECES,)),
        ],
        compiler_params=params(),
        name="unpack",
    )(back)


def body(field_state, zonal_taps, channel_mix, channel_bias):
    lon_count = lax.axis_size("lon")
    ch_count = lax.axis_size("ch")
    width, depth, lats = field_state.shape
    sent = pack(field_state.reshape(width * depth, lats), width, depth)
    got = exchange(sent.reshape(lats, ROWS, 2 * depth)).reshape(sent.shape)
    answer = filter_mix(got, zonal_taps, channel_mix, channel_bias, lon_count, ch_count, width)
    back = exchange(answer.reshape(lats, ROWS, 2 * depth)).reshape(sent.shape)
    return unpack(back, width, depth, lats).reshape(width, depth, lats)


def solution(mesh):
    placed = (P("lon", "ch", None), P(), P(), P())
    return jax.shard_map(
        body, mesh=mesh, in_specs=placed, out_specs=P("lon", "ch", None), check_vma=False
    )
```

time: 118 us -> 115 us (0.975)
  blocking collectives: 48.3 us -> 106 us
  waiting for transfers between devices: 38.6 us -> 0 us
  starting transfers between devices: 15.7 us -> 0 us
  local copies, waits for them, and re-layouts: 5.93 us -> 1.39 us
  Pallas kernels: 9.26 us -> 7.76 us
    all_to_all x1 -> x2, blocking collectives: 48.3 us -> 106 us  [exchange(): lax.all_to_all(x, ('lon', 'ch'), split_axis=0, concat_axis=0, tiled=True)]
    all_to_all x1 -> x0, waiting for transfers between devices: 38.6 us -> none  [exchange(): lax.all_to_all(x, ('lon', 'ch'), split_axis=0, concat_axis=0, tiled=True)]
    all_to_all x1 -> x0, starting transfers between devices: 15.7 us -> none  [exchange(): lax.all_to_all(x, ('lon', 'ch'), split_axis=0, concat_axis=0, tiled=True)]
    unnamed x17 -> x8, local copies, waits for them, and re-layouts: 5.6 us -> 1.39 us
    pallas_call x4 -> x3, Pallas kernels: 9.26 us -> 7.76 us  [the longest x1 4.96 us: filter_mix(): pl.pallas_call(lambda *refs: filter_kernel(lon_count, ch_count, width, le...]
  transfers between devices with their start and end apart: 1 -> 0, of which waited for: 1 -> 0; matrix products, arithmetic and copies ran while one was open for 2% -> 0% of each run, Pallas kernels for 0% -> 0%
where the time goes in v1:
time: 115 us
  blocking collectives  106 us (92%)
  Pallas kernels  7.76 us (7%)
  local copies, waits for them, and re-layouts  1.39 us (1%)
    all_to_all x2, blocking collectives, exchange(): lax.all_to_all(x, ('lon', 'ch'), split_axis=0, concat_axis=0, tiled=True)  106 us
    pallas_call x1, Pallas kernels, filter_mix(): pl.pallas_call(lambda *refs: filter_kernel(lon_count, ch_count, width, le...  4.96 us

profile of v1, /device:TPU:1, one launch (start us, length us, event | category | flops | bytes accessed | tf_op | source)
XLA Modules:
  0.0 115.0 jit_solution(15737007403488536196)
XLA Ops:
  0.0 0.0 copy-start
  0.0 1.4 %copy-done = bf16[45,64,256]{2,1,0:T(8,128)(2,1)S(1)} copy-done((bf16[45,64,256]{2,1,0:T(8,128)(2,1)S(1)}, bf16[45,64,256]{2,1,0:T(8,128)(2,1)}, u32[]{:S(2)}) %copy-start) | copy-done | bytes 1474584
  1.4 1.1 pack.1
  2.4 0.0 copy-start.1
  2.4 0.0 copy-start.2
  2.5 0.0 copy-start.3
  2.5 57.5 %all_to_all.10 = bf16[256,24,128]{2,1,0:T(8,128)(2,1)S(1)} all-to-all(bf16[256,24,128]{2,1,0:T(8,128)(2,1)S(1)} %bitcast.9), channel_id=1, replica_groups=mesh['lon'=32,'ch'=8] {'lon','ch'}, dimensions={0} | all-to-all | bytes 3145728 | tf_op jit(solution)/shard_map/all_to_all | solution.py:145
  60.0 0.0 copy-done.1
  60.0 0.0 copy-done.2
  60.0 0.0 copy-done.3
  60.0 5.0 %filter_mix.1 = bf16[6144,128]{1,0:T(8,128)(2,1)S(1)} custom-call(bf16[6144,128]{1,0:T(8,128)(2,1)S(1)} %bitcast.10, bf16[1440,256]{1,0:T(8,128)(2,1)S(1)} %bitcast.13, bf16[512,512]{1,0:T(8,128)(2,1)S(1)} %copy-done.2, f32[1,512]{1,0:T(1,128)S(1)} %bitcast.14), custom_call_target="tpu_custom_call" | custom-call | tf_op jit(solution)/shard_map/filter_mix/pallas_call | solution.py:163
  65.0 48.3 %all_to_all.11 = bf16[256,24,128]{2,1,0:T(8,128)(2,1)S(1)} all-to-all(bf16[256,24,128]{2,1,0:T(8,128)(2,1)S(1)} %bitcast.11), channel_id=1, replica_groups=mesh['lon'=32,'ch'=8] {'lon','ch'}, dimensions={0} | all-to-all | bytes 3145728 | tf_op jit(solution)/shard_map/all_to_all | solution.py:145
  113.3 1.8 %unpack.1 = bf16[2880,256]{1,0:T(8,128)(2,1)} custom-call(bf16[6144,128]{1,0:T(8,128)(2,1)S(1)} %bitcast.8), custom_call_target="tpu_custom_call" | custom-call | tf_op jit(solution)/shard_map/unpack/pallas_call | solution.py:178
Async XLA Ops:
  0.0 1.4 %copy-start = (bf16[45,64,256]{2,1,0:T(8,128)(2,1)S(1)}, bf16[45,64,256]{2,1,0:T(8,128)(2,1)}, u32[]{:S(2)}) copy-start(bf16[45,64,256]{2,1,0:T(8,128)(2,1)} %param.4) | copy-start | bytes 4423684
  2.4 57.6 %copy-start.1 = (bf16[256,1440]{0,1:T(8,128)(2,1)S(1)}, bf16[256,1440]{0,1:T(8,128)(2,1)}, u32[]{:S(2)}) copy-start(bf16[256,1440]{0,1:T(8,128)(2,1)} %param.5) | copy-start | bytes 2211844
  2.4 57.6 %copy-start.2 = (bf16[512,512]{1,0:T(8,128)(2,1)S(1)}, bf16[512,512]{1,0:T(8,128)(2,1)}, u32[]{:S(2)}) copy-start(bf16[512,512]{1,0:T(8,128)(2,1)} %refs_2_.1) | copy-start | bytes 1572868
  2.5 57.6 %copy-start.3 = (f32[512]{0:T(512)S(1)}, f32[512]{0:T(512)}, u32[]{:S(2)}) copy-start(f32[512]{0:T(512)} %param.7) | copy-start | bytes 6148

commit v2 on v1

--- a/solution.py
+++ b/solution.py
@@ -7,9 +7,9 @@
 
 HALF = 23
 ROWS = 24
-TALL = 256
+TALL = 384
 LIMIT = 40 * 1024 * 1024
-PIECES = 4
+PIECES = 6
 
 
 def params():
@@ -96,7 +96,7 @@
 
 
 def filter_kernel(
-    lon_count, ch_count, width, length, x_ref, turned_ref, mix_ref, bias_ref, out_ref, strip, state, packed, result
+    lon_count, ch_count, width, length, x_ref, turned_ref, mix_ref, bias_ref, out_ref, strip, state, packed, result, half
 ):
     channels = state.shape[1]
     half_lanes = 64
@@ -108,8 +108,12 @@
     base = jnp.broadcast_to(line[0:1, :], (TALL, line.shape[1]))
     strip[...] = pltpu.roll(base, 0, 1, stride=1, stride_axis=0)[:, TALL:].astype(strip.dtype)
     low = lax.broadcasted_iota(jnp.int32, (ROWS, 128), 1) < half_lanes
-    for l in range(lon_count):
-        for pair in range(ch_count // 2):
+    padded = state.shape[0]
+    pairs = ch_count // 2
+    sides = [slice(0, channels // 2), slice(channels // 2, channels)]
+
+    def take(l, side):
+        for pair in range(side * pairs // 2, (side + 1) * pairs // 2):
             at = (l * ch_count + 2 * pair) * ROWS
             first = x_ref[at : at + ROWS, :].astype(jnp.float32)
             second = x_ref[at + ROWS : at + 2 * ROWS, :].astype(jnp.float32)
@@ -118,18 +122,27 @@
             state[l * width + HALF : l * width + HALF + ROWS, lanes] = jnp.where(
                 low, pltpu.roll(first, half_lanes, 1), second
             )
-    padded = state.shape[0]
-    packed[...] = state[...].astype(jnp.bfloat16)
-    packed[length:, :] = jnp.zeros((padded - length, channels), jnp.bfloat16)
-    result[length:, :] = jnp.zeros((result.shape[0] - length, channels), jnp.float32)
-    for start in range(0, length, TALL):
-        count = min(TALL, length - start)
+
+    def close(side):
+        packed[:length, sides[side]] = state[:length, sides[side]].astype(jnp.bfloat16)
+        packed[length:, sides[side]] = jnp.zeros((padded - length, channels // 2), jnp.bfloat16)
+
+    def filtered_block(block, side):
+        start, count = block
         offset = (length // 128) * 128 - start
         taps = strip[:count, offset : offset + padded]
-        filtered = jnp.dot(taps, packed[...], preferred_element_type=jnp.float32).astype(jnp.bfloat16)
+        return jnp.dot(taps, packed[:, sides[side]], preferred_element_type=jnp.float32).astype(jnp.bfloat16)
+
+    for l in range(lon_count):
+        take(l, 0)
+    close(0)
+    result[length:, :] = jnp.zeros((result.shape[0] - length, channels), jnp.float32)
+
+    def finish(start, filtered):
         mixed = jnp.dot(filtered, mix_ref[...], preferred_element_type=jnp.float32) + bias_ref[...]
-        result[start : start + count, :] = mixed / (1.0 + jnp.exp(-mixed))
-    for l in range(lon_count):
+        result[start : start + filtered.shape[0], :] = mixed / (1.0 + jnp.exp(-mixed))
+
+    def send(l):
         for pair in range(ch_count // 2):
             lanes = slice(pair * 128, (pair + 1) * 128)
             first = result[l * width : l * width + ROWS, lanes]
@@ -139,6 +152,30 @@
             out_ref[at + ROWS : at + 2 * ROWS, :] = jnp.where(low, pltpu.roll(first, half_lanes, 1), second).astype(
                 out_ref.dtype
             )
+
+    blocks = [(start, min(TALL, length - start)) for start in range(0, length, TALL)]
+    taken = 0
+    for i, block in enumerate(blocks):
+        half[block[0] : block[0] + block[1], :] = filtered_block(block, 0)
+        upto = lon_count * (i + 1) // len(blocks)
+        for l in range(taken, upto):
+            take(l, 1)
+        taken = upto
+    close(1)
+    waiting = None
+    sent = 0
+    for stage in range(len(blocks) + 2):
+        if stage < len(blocks):
+            start, count = blocks[stage]
+            latest = jnp.concatenate([half[start : start + count, :], filtered_block(blocks[stage], 1)], 1)
+        if 1 <= stage <= len(blocks):
+            finish(blocks[stage - 1][0], waiting)
+        waiting = latest
+        if stage >= 2:
+            known = blocks[stage - 2][0] + blocks[stage - 2][1]
+            while sent < lon_count and (known >= length or sent * width + HALF + ROWS <= known):
+                send(sent)
+                sent += 1
 
 
 def exchange(x):
@@ -168,6 +205,7 @@
             pltpu.VMEM((padded, channels), jnp.float32),
             pltpu.VMEM((padded, channels), jnp.bfloat16),
             pltpu.VMEM((padded, channels), jnp.float32),
+            pltpu.VMEM((padded, channels // 2), jnp.bfloat16),
         ],
         compiler_params=params(),
         name="filter_mix",

time: 115 us -> 115 us (level)
  no operation moved by 1% of the time
where the time goes in v2:
time: 115 us
  blocking collectives  106 us (92%)
  Pallas kernels  7.55 us (7%)
  local copies, waits for them, and re-layouts  1.39 us (1%)
    all_to_all x2, blocking collectives, exchange(): lax.all_to_all(x, ('lon', 'ch'), split_axis=0, concat_axis=0, tiled=True)  106 us
    pallas_call x1, Pallas kernels, filter_mix(): pl.pallas_call(lambda *refs: filter_kernel(lon_count, ch_count, width, le...  4.76 us

profile of v2, /device:TPU:1, one launch (start us, length us, event | category | flops | bytes accessed | tf_op | source)
XLA Modules:
  0.0 114.8 jit_solution(8869933161945865598)
XLA Ops:
  0.0 0.0 copy-start
  0.0 1.4 %copy-done = bf16[45,64,256]{2,1,0:T(8,128)(2,1)S(1)} copy-done((bf16[45,64,256]{2,1,0:T(8,128)(2,1)S(1)}, bf16[45,64,256]{2,1,0:T(8,128)(2,1)}, u32[]{:S(2)}) %copy-start) | copy-done | bytes 1474584
  1.4 1.1 pack.1
  2.4 0.0 copy-start.1
  2.4 0.0 copy-start.2
  2.5 0.0 copy-start.3
  2.5 57.5 %all_to_all.10 = bf16[256,24,128]{2,1,0:T(8,128)(2,1)S(1)} all-to-all(bf16[256,24,128]{2,1,0:T(8,128)(2,1)S(1)} %bitcast.9), channel_id=1, replica_groups=mesh['lon'=32,'ch'=8] {'lon','ch'}, dimensions={0} | all-to-all | bytes 3145728 | tf_op jit(solution)/shard_map/all_to_all | solution.py:182
  60.0 0.0 copy-done.1
  60.0 0.0 copy-done.2
  60.0 0.0 copy-done.3
  60.0 4.8 %filter_mix.1 = bf16[6144,128]{1,0:T(8,128)(2,1)S(1)} custom-call(bf16[6144,128]{1,0:T(8,128)(2,1)S(1)} %bitcast.10, bf16[1440,256]{1,0:T(8,128)(2,1)S(1)} %bitcast.13, bf16[512,512]{1,0:T(8,128)(2,1)S(1)} %copy-done.2, f32[1,512]{1,0:T(1,128)S(1)} %bitcast.14), custom_call_target="tpu_custom_call" | custom-call | tf_op jit(solution)/shard_map/filter_mix/pallas_call | solution.py:200
  64.8 48.3 %all_to_all.11 = bf16[256,24,128]{2,1,0:T(8,128)(2,1)S(1)} all-to-all(bf16[256,24,128]{2,1,0:T(8,128)(2,1)S(1)} %bitcast.11), channel_id=1, replica_groups=mesh['lon'=32,'ch'=8] {'lon','ch'}, dimensions={0} | all-to-all | bytes 3145728 | tf_op jit(solution)/shard_map/all_to_all | solution.py:182
  113.1 1.7 %unpack.1 = bf16[2880,256]{1,0:T(8,128)(2,1)} custom-call(bf16[6144,128]{1,0:T(8,128)(2,1)S(1)} %bitcast.8), custom_call_target="tpu_custom_call" | custom-call | tf_op jit(solution)/shard_map/unpack/pallas_call | solution.py:216
Async XLA Ops:
  0.0 1.4 %copy-start = (bf16[45,64,256]{2,1,0:T(8,128)(2,1)S(1)}, bf16[45,64,256]{2,1,0:T(8,128)(2,1)}, u32[]{:S(2)}) copy-start(bf16[45,64,256]{2,1,0:T(8,128)(2,1)} %param.4) | copy-start | bytes 4423684
  2.4 57.6 %copy-start.1 = (bf16[256,1440]{0,1:T(8,128)(2,1)S(1)}, bf16[256,1440]{0,1:T(8,128)(2,1)}, u32[]{:S(2)}) copy-start(bf16[256,1440]{0,1:T(8,128)(2,1)} %param.5) | copy-start | bytes 2211844
  2.4 57.6 %copy-start.2 = (bf16[512,512]{1,0:T(8,128)(2,1)S(1)}, bf16[512,512]{1,0:T(8,128)(2,1)}, u32[]{:S(2)}) copy-start(bf16[512,512]{1,0:T(8,128)(2,1)} %refs_2_.1) | copy-start | bytes 1572868
  2.5 57.6 %copy-start.3 = (f32[512]{0:T(512)S(1)}, f32[512]{0:T(512)}, u32[]{:S(2)}) copy-start(f32[512]{0:T(512)} %param.7) | copy-start | bytes 6148
